TPU v7x, 32 devices: a whole 2x2x4 slice. The times are simulated.
32 devices in a mesh: ctx: 16 (over z, y, x), head: 2 (over core).
Axes of the slice: x: 2, y: 2, z: 4, core: 2. Of those that a mesh axis runs over, the one named last changes fastest.
Arguments:
- queries: bfloat16 [4096, 1024], P('ctx', 'head'), may hold values from -10 to 10
- keys: bfloat16 [4096, 128], P('ctx'), may hold values from -6 to 6
- values: bfloat16 [4096, 128], P('ctx'), may hold values from -6 to 6
- doc_lengths: int32 [4], replicated, may hold values from 1 to 3072, 4096 in all
Outputs:
- attn_rows: bfloat16 [4096, 1024], P('ctx', 'head')
- col_scores: float32 [4096], P(('ctx', 'head'))
Inputs may be any that keep to these rules, and one draw needn't show every extreme that they name: `doc_lengths`: the 4 lengths sum to 4096 and the longest is exactly 3072.
All inputs are finite; a program needn't handle non-finite values.
Results may differ from a plain program's by a relative error of at most 0.0075.
Values may be sent and summed in bfloat16 or wider, within the bound.
A program may use at most 64 MiB of HBM per device.

v0:
```python
import functools
import math

import jax
import jax.numpy as jnp
from jax import lax
from jax.experimental import pallas as pl
from jax.experimental.pallas import tpu as pltpu
from jax.sharding import PartitionSpec as P

HD = 128
HEADS = 8
PLANE = 4
BIG = 32768.0
MESH = pl.DeviceIdType.MESH
SCALE = math.log2(math.e) / math.sqrt(HD)


def place(planes):
    me, core = lax.axis_index("ctx"), lax.axis_index("head")
    return me, core, me // PLANE, me % PLANE


def remote(src, dst, send, recv, ctx, core):
    return pltpu.make_async_remote_copy(
        src_ref=src,
        dst_ref=dst,
        send_sem=send,
        recv_sem=recv,
        device_id={"ctx": ctx, "head": core},
        device_id_type=MESH,
    )


class Gather:
    def __init__(self, planes, cores, kv, send, recv, sib_send, sib_recv):
        self.planes, self.cores, self.kv = planes, cores, kv
        self.send, self.recv = send, recv
        self.sib_send, self.sib_recv = sib_send, sib_recv
        self.me, self.core, self.z, self.p = place(planes)
        self.px = self.p + 1 - 2 * (self.p % 2)
        self.py = (self.p + 2) % PLANE
        self.pd = (self.px + 2) % PLANE
        self.xn = self.z * PLANE + self.px
        self.yn = self.z * PLANE + self.py

    def block(self, s, which):
        return (self.z - s) * PLANE + (self.p, self.px, self.py, self.pd)[which]

    def ref(self, s, kind, core):
        if kind < 3:
            return self.kv.at[self.block(s, kind), core]
        return self.kv.at[self.block(s, 3), core, 4 - kind]

    def chain_copy(self, s):
        ref = self.ref(s, 0, self.core)
        return remote(ref, ref, self.send.at[0, s], self.recv.at[0, s + 1], self.me + PLANE, self.core)

    def plane_copy(self, s, kind):
        ref = self.ref(s, 0, self.core)
        if kind == 3:
            ref = self.kv.at[self.block(s, 1), self.core, 1]
        if kind == 4:
            ref = self.kv.at[self.block(s, 2), self.core, 0]
        to = self.xn if kind in (1, 4) else self.yn
        return remote(ref, ref, self.send.at[kind, s], self.recv.at[kind, s], to, self.core)

    def sib_copy(self, s, kind, step):
        ref = self.ref(s, kind, self.core)
        return remote(
            ref,
            ref,
            self.sib_send.at[kind, step - 1, s],
            self.sib_recv.at[kind, step - 1, s],
            self.me,
            (self.core + step) % self.cores,
        )

    def wait_arrival(self, s, kind):
        ref = self.ref(s, kind, self.core)
        remote(ref, ref, self.send.at[kind, s], self.recv.at[kind, s], self.xn, self.core).wait_recv()

    def sibs(self, s, kind):
        for step in range(1, self.cores):
            self.sib_copy(s, kind, step).start()

    def chain(self, s, own=False):
        @pl.when(s <= self.z)
        def _():
            if not own:
                self.wait_arrival(s, 0)
            pl.when(self.z < self.planes - 1)(lambda: self.chain_copy(s).start())
            self.plane_copy(s, 1).start()
            self.plane_copy(s, 2).start()
            if not own:
                self.sibs(s, 0)

    def cross(self, s):
        @pl.when(s <= self.z)
        def _():
            self.wait_arrival(s, 1)
            self.plane_copy(s, 3).start()
            self.sibs(s, 1)
            self.wait_arrival(s, 2)
            self.plane_copy(s, 4).start()
            self.sibs(s, 2)

    def diagonal(self, s):
        @pl.when(s <= self.z)
        def _():
            for kind in (4, 3):
                self.wait_arrival(s, kind)
                self.sibs(s, kind)

    def landed(self, s, kind):
        for step in range(1, self.cores):
            ref = self.ref(s, kind, (self.core + self.cores - step) % self.cores)
            remote(
                ref,
                ref,
                self.sib_send.at[kind, step - 1, s],
                self.sib_recv.at[kind, step - 1, s],
                self.me,
                (self.core + step) % self.cores,
            ).wait_recv()

    def sent(self, s, own=False):
        pl.when(self.z < self.planes - 1)(lambda: self.chain_copy(s).wait_send())
        for kind in range(5):
            if kind > 0:
                self.plane_copy(s, kind).wait_send()
            if kind > 0 or not own:
                for step in range(1, self.cores):
                    self.sib_copy(s, kind, step).wait_send()


def gather_sems(planes, cores):
    return [
        pltpu.SemaphoreType.DMA((5, planes)),
        pltpu.SemaphoreType.DMA((5, planes)),
        pltpu.SemaphoreType.DMA((5, max(cores - 1, 1), planes)),
        pltpu.SemaphoreType.DMA((5, max(cores - 1, 1), planes)),
    ]


def doc_of(ends, start, shape):
    position = start + lax.broadcasted_iota(jnp.int32, shape, 0)
    result = jnp.zeros(shape, jnp.int32)
    for end in ends:
        result += (position >= end).astype(jnp.int32)
    return result


def kernel(planes, cores, docs_ref, q_hbm, k_hbm, v_hbm, rows_hbm, out_ref, *scratch):
    q_ref, kv, qx, s_ref, p_ref, mx_ref, m_ref, acc, o_ref, comb, cols_ref, held, mid, late = scratch[:14]
    load, store, send, recv, zsend, zrecv = scratch[14:20]
    g = Gather(planes, cores, kv, *scratch[20:])
    me, core, z, p = g.me, g.core, g.z, g.p
    tok, heads = q_ref.shape[0], q_ref.shape[1] // HD
    width = tok // cores
    span = PLANE * tok
    steps = [(a, c) for a in range(PLANE) for c in range(cores) if (a, c) != (0, 0)]

    loads = [pltpu.make_async_copy(q_hbm, q_ref, load.at[2 * cores])]
    for part in range(cores):
        rows = pl.ds(part * width, width)
        loads.append(pltpu.make_async_copy(k_hbm.at[rows], kv.at[me, part, 0], load.at[2 * part]))
        loads.append(pltpu.make_async_copy(v_hbm.at[rows], kv.at[me, part, 1], load.at[2 * part + 1]))
    for copy in loads[1:] + loads[:1]:
        copy.start()

    sem = pltpu.get_barrier_semaphore()

    def tell(ctx, to):
        pl.semaphore_signal(sem, inc=1, device_id={"ctx": ctx, "head": to}, device_id_type=MESH)

    for a, c in steps:
        tell(z * PLANE + (p + a) % PLANE, (core + c) % cores)
    for step in range(1, planes):
        tell((z + step) % planes * PLANE + p, core)
    for copy in loads[1:]:
        copy.wait()
    pl.semaphore_wait(sem, len(steps) + planes - 1)
    g.chain(0, own=True)

    ends, total = [], 0
    for i in range(docs_ref.shape[0]):
        total = total + docs_ref[i]
        ends.append(total)
    lane = lax.broadcasted_iota(jnp.int32, (tok, HD), 1)
    mark = jnp.where(lane == doc_of(ends, me * tok, (tok, HD)), 1.0, 0.0).astype(jnp.bfloat16)
    loads[0].wait()
    for h in range(heads):
        qx[h, :, :HD] = q_ref[:, h * HD : (h + 1) * HD]
        qx[h, :, HD:] = mark
    cols_ref[...] = jnp.zeros_like(cols_ref)
    comb[...] = jnp.zeros_like(comb)
    ones = jnp.ones((tok, HD), jnp.bfloat16)
    row = lax.broadcasted_iota(jnp.int32, (tok, tok), 0)
    col = lax.broadcasted_iota(jnp.int32, (tok, tok), 1)

    def whole(b, which):
        return jnp.concatenate([kv[b, c, which] for c in range(cores)], axis=0)

    def scan(s, which, own):
        b = g.block(s, which)
        bar = jnp.where(lane == doc_of(ends, b * tok, (tok, HD)), 0.0, -BIG).astype(jnp.bfloat16)
        kx = jnp.concatenate([whole(b, 0), bar], axis=1)
        for h in range(heads):
            x = lax.dot_general(qx[h], kx, (((1,), (1,)), ((), ())), preferred_element_type=jnp.float32)
            if own:
                x = jnp.where(col + (b - me) * tok <= row, x, -BIG)
            s_ref[h, :, which * tok : (which + 1) * tok] = x
            top = x[:, :HD]
            for i in range(1, tok // HD):
                top = jnp.maximum(top, x[:, i * HD : (i + 1) * HD])
            mx_ref[h] = top if which == 0 else jnp.maximum(mx_ref[h], top)

    def weigh(s, h, own):
        top = jnp.broadcast_to(jnp.max(mx_ref[h], axis=1, keepdims=True) * SCALE, (tok, HD))
        if not own:
            old = m_ref[s - 1, h]
            top = jnp.maximum(old, top)
            fade = jnp.exp2(old - top)
        m_ref[s, h] = top
        wide = jnp.concatenate([top] * (tok // HD), axis=1)
        for which in range(PLANE):
            part = slice(which * tok, (which + 1) * tok)
            p_ref[s, h, :, part] = jnp.exp2(s_ref[h, :, part] * SCALE - wide).astype(jnp.bfloat16)
        vx = jnp.concatenate(
            [jnp.concatenate([whole(g.block(s, which), 1), ones], axis=1) for which in range(PLANE)], axis=0
        )
        new = jnp.dot(p_ref[s, h], vx, preferred_element_type=jnp.float32)
        if not own:
            new += acc[h] * jnp.concatenate([fade, fade], axis=1)
        acc[h] = new

    def one_round(s, own):
        if not own:
            g.landed(s, 0)
            scan(s, 0, own)
        g.landed(s, 1)
        scan(s, 1, own)
        g.chain(s + 2)
        g.landed(s, 2)
        scan(s, 2, own)
        g.cross(s + 1)
        g.landed(s, 4)
        g.landed(s, 3)
        scan(s, 3, own)
        for h in range(heads):
            weigh(s, h, own)
            if h == heads // 2:
                g.diagonal(s + 1)

    scan(0, 0, True)
    g.chain(1)
    g.cross(0)
    g.diagonal(0)
    one_round(0, True)

    @pl.loop(1, z + 1)
    def _(s):
        one_round(s, False)

    for h in range(heads):
        inverse = 1.0 / acc[h, :, HD:]
        o_ref[:, h * HD : (h + 1) * HD] = (acc[h, :, :HD] * inverse).astype(o_ref.dtype)
        acc[h, :, HD:] = inverse

    @pl.loop(0, z + 1)
    def _(s):
        for h in range(heads):
            weight = jnp.exp2(m_ref[s, h] - m_ref[z, h]) * acc[h, :, HD:]
            comb[...] = jnp.where(lane == s * heads + h, weight, comb[...])

    out_copy = pltpu.make_async_copy(o_ref, rows_hbm, store.at[0])
    out_copy.start()
    across = jnp.transpose(comb[...])
    held_rows = mx_ref
    for half in range(tok // HD):
        held_rows[0, half * HD : (half + 1) * HD, :] = across[:, half * HD : (half + 1) * HD]
    line = lax.broadcasted_iota(jnp.int32, (16, tok), 0)

    @pl.loop(0, z + 1)
    def _(s):
        sums = jnp.zeros((16, span), jnp.float32)
        for h in range(heads):
            w = jnp.concatenate(
                [held_rows[0, pl.ds(half * HD + s * heads + h, 1), :] for half in range(tok // HD)], axis=1
            )
            w = jnp.broadcast_to(w, (16, tok))
            high = w.astype(jnp.bfloat16).astype(jnp.float32)
            w = jnp.where(line == 0, high, jnp.where(line == 1, w - high, 0.0)).astype(jnp.bfloat16)
            sums += jnp.dot(w, p_ref[s, h], preferred_element_type=jnp.float32)
        sums = jnp.sum(sums, axis=0, keepdims=True)
        for which in range(PLANE):
            b = g.block(s, which)
            for c in range(cores):
                start = which * tok + c * width
                cols_ref[b % PLANE, c, b // PLANE] = sums[:, start : start + width]

    def plane_copy(n):
        a, c = steps[n]
        pn, cn = (p + a) % PLANE, (core + c) % cores
        return remote(cols_ref.at[pn, cn], held.at[n], send.at[n], recv.at[n], z * PLANE + pn, cn)

    for n in range(len(steps)):
        plane_copy(n).start()
    g.sent(0, own=True)

    @pl.loop(1, z + 1)
    def _(s):
        g.sent(s)

    total = cols_ref[p, core]
    for n in range(len(steps)):
        plane_copy(n).wait_recv()
        total += held[n]
    mid[...] = total

    def z_copy(step):
        to = (z + step) % planes
        return remote(mid.at[to], late.at[step], zsend.at[step], zrecv.at[step], to * PLANE + p, core)

    for step in range(1, planes):
        z_copy(step).start()
    result = mid[z]
    for step in range(1, planes):
        z_copy(step).wait_recv()
        result += late[step]
    out_ref[...] = result * (1.0 / HEADS)
    for n in range(len(steps)):
        plane_copy(n).wait_send()
    for step in range(1, planes):
        z_copy(step).wait_send()
    out_copy.wait()


def body(planes, cores, queries, keys, values, doc_lengths):
    tok, heads = queries.shape[0], queries.shape[1] // HD
    ctx, width = planes * PLANE, tok // cores
    partners = PLANE * cores - 1
    anywhere = pl.BlockSpec(memory_space=pl.ANY)
    rows, scores = pl.pallas_call(
        functools.partial(kernel, planes, cores),
        out_shape=(
            jax.ShapeDtypeStruct(queries.shape, jnp.bfloat16),
            jax.ShapeDtypeStruct((1, width), jnp.float32),
        ),
        in_specs=[pl.BlockSpec(memory_space=pltpu.SMEM), anywhere, anywhere, anywhere],
        out_specs=(anywhere, pl.BlockSpec(memory_space=pltpu.VMEM)),
        scratch_shapes=[
            pltpu.VMEM(queries.shape, jnp.bfloat16),
            pltpu.VMEM((ctx, cores, 2, width, HD), jnp.bfloat16),
            pltpu.VMEM((heads, tok, 2 * HD), jnp.bfloat16),
            pltpu.VMEM((heads, tok, PLANE * tok), jnp.float32),
            pltpu.VMEM((planes, heads, tok, PLANE * tok), jnp.bfloat16),
            pltpu.VMEM((heads, tok, HD), jnp.float32),
            pltpu.VMEM((planes, heads, tok, HD), jnp.float32),
            pltpu.VMEM((heads, tok, 2 * HD), jnp.float32),
            pltpu.VMEM(queries.shape, jnp.bfloat16),
            pltpu.VMEM((tok, HD), jnp.float32),
            pltpu.VMEM((PLANE, cores, planes, 1, width), jnp.float32),
            pltpu.VMEM((partners, planes, 1, width), jnp.float32),
            pltpu.VMEM((planes, 1, width), jnp.float32),
            pltpu.VMEM((planes, 1, width), jnp.float32),
            pltpu.SemaphoreType.DMA((2 * cores + 1,)),
            pltpu.SemaphoreType.DMA((1,)),
            pltpu.SemaphoreType.DMA((partners,)),
            pltpu.SemaphoreType.DMA((partners,)),
            pltpu.SemaphoreType.DMA((planes,)),
            pltpu.SemaphoreType.DMA((planes,)),
        ]
        + gather_sems(planes, cores),
        compiler_params=pltpu.CompilerParams(
            collective_id=0, has_side_effects=True, vmem_limit_bytes=62 * 1024 * 1024
        ),
        name="attend",
    )(doc_lengths, queries, keys, values)
    return rows, scores.reshape(width)


def solution(mesh):
    planes, cores = mesh.shape["ctx"] // PLANE, mesh.shape["head"]
    return jax.shard_map(
        functools.partial(body, planes, cores),
        mesh=mesh,
        in_specs=(P("ctx", "head"), P("ctx", None), P("ctx", None), P()),
        out_specs=(P("ctx", "head"), P(("ctx", "head"))),
        check_vma=False,
    )
```

profile of v0, /device:TPU:0, one launch (start us, length us, event | category | flops | bytes accessed | tf_op | source)
XLA Modules:
  0.0 42.0 jit_solution(10810914990765901678)
XLA Ops:
  0.6 39.2 %attend.1 = (bf16[256,512]{1,0:T(8,128)(2,1)}, f32[1,128]{1,0:T(1,128)}) custom-call(s32[4]{0:T(128)} %docs_ref.1, bf16[256,512]{1,0:T(8,128)(2,1)} %q_hbm.1, bf16[256,128]{1,0:T(8,128)(2,1)} %k_hbm.1, bf16[256,128]{1,0:T(8,128)(2,1)} %v_hbm.1), custom_call_target="tpu_custom_call" | custom-call | tf_op jit(solution)/shard_map/attend/pallas_call | solution.py:345
  39.8 0.0 copy-start
  39.8 1.7 %copy.8 = bf16[256,512]{1,0:T(8,128)(2,1)} copy(bf16[256,512]{1,0:T(8,128)(2,1)} %get-tuple-element.8) | data formatting | bytes 524288
  41.5 0.0 copy-done
  41.5 0.5 %copy.9 = f32[128]{0:T(128)} copy(f32[128]{0:T(128)S(1)} %bitcast.1) | data formatting | bytes 1024
Async XLA Ops:
  39.8 1.7 %copy-start = (f32[1,128]{1,0:T(1,128)S(1)}, f32[1,128]{1,0:T(1,128)}, u32[]{:S(2)}) copy-start(f32[1,128]{1,0:T(1,128)} %get-tuple-element.5) | copy-start | bytes 1540
where the time goes:
time: 42.2 us; the launch traced here: 42 us
  Pallas kernels  39.2 us (93%)
  local copies, waits for them, and re-layouts  2.19 us (5%)
  between operations  0.65 us (2%)
    pallas_call x1, Pallas kernels, body(): pl.pallas_call(functools.partial(kernel, planes, cores), out_shape=(jax.S...  39.2 us
    unnamed x4, local copies, waits for them, and re-layouts  2.19 us

commit v1 on v0

--- a/solution.py
+++ b/solution.py
@@ -85,17 +85,24 @@
             self.sib_copy(s, kind, step).start()
 
     def chain(self, s, own=False):
+        if s >= self.planes:
+            return
+
         @pl.when(s <= self.z)
         def _():
             if not own:
                 self.wait_arrival(s, 0)
-            pl.when(self.z < self.planes - 1)(lambda: self.chain_copy(s).start())
+            if s < self.planes - 1:
+                pl.when(self.z < self.planes - 1)(lambda: self.chain_copy(s).start())
             self.plane_copy(s, 1).start()
             self.plane_copy(s, 2).start()
             if not own:
                 self.sibs(s, 0)
 
     def cross(self, s):
+        if s >= self.planes:
+            return
+
         @pl.when(s <= self.z)
         def _():
             self.wait_arrival(s, 1)
@@ -106,6 +113,9 @@
             self.sibs(s, 2)
 
     def diagonal(self, s):
+        if s >= self.planes:
+            return
+
         @pl.when(s <= self.z)
         def _():
             for kind in (4, 3):
@@ -210,15 +220,15 @@
             x = lax.dot_general(qx[h], kx, (((1,), (1,)), ((), ())), preferred_element_type=jnp.float32)
             if own:
                 x = jnp.where(col + (b - me) * tok <= row, x, -BIG)
-            s_ref[h, :, which * tok : (which + 1) * tok] = x
+            s_ref[s % 2, h, :, which * tok : (which + 1) * tok] = x
             top = x[:, :HD]
             for i in range(1, tok // HD):
                 top = jnp.maximum(top, x[:, i * HD : (i + 1) * HD])
-            mx_ref[h] = top if which == 0 else jnp.maximum(mx_ref[h], top)
-
-    def weigh(s, h, own):
-        top = jnp.broadcast_to(jnp.max(mx_ref[h], axis=1, keepdims=True) * SCALE, (tok, HD))
-        if not own:
+            mx_ref[s % 2, h] = top if which == 0 else jnp.maximum(mx_ref[s % 2, h], top)
+
+    def weigh(s, h):
+        top = jnp.broadcast_to(jnp.max(mx_ref[s % 2, h], axis=1, keepdims=True) * SCALE, (tok, HD))
+        if s > 0:
             old = m_ref[s - 1, h]
             top = jnp.maximum(old, top)
             fade = jnp.exp2(old - top)
@@ -226,42 +236,49 @@
         wide = jnp.concatenate([top] * (tok // HD), axis=1)
         for which in range(PLANE):
             part = slice(which * tok, (which + 1) * tok)
-            p_ref[s, h, :, part] = jnp.exp2(s_ref[h, :, part] * SCALE - wide).astype(jnp.bfloat16)
+            p_ref[s, h, :, part] = jnp.exp2(s_ref[s % 2, h, :, part] * SCALE - wide).astype(jnp.bfloat16)
         vx = jnp.concatenate(
             [jnp.concatenate([whole(g.block(s, which), 1), ones], axis=1) for which in range(PLANE)], axis=0
         )
         new = jnp.dot(p_ref[s, h], vx, preferred_element_type=jnp.float32)
-        if not own:
+        if s > 0:
             new += acc[h] * jnp.concatenate([fade, fade], axis=1)
         acc[h] = new
 
-    def one_round(s, own):
-        if not own:
+    def step(s, which):
+        scan(s, which, s == 0)
+        if s > 0:
+            for h in range(which, heads, PLANE):
+                weigh(s - 1, h)
+
+    def one_round(s):
+        if s > 0:
             g.landed(s, 0)
-            scan(s, 0, own)
+            step(s, 0)
         g.landed(s, 1)
-        scan(s, 1, own)
+        step(s, 1)
         g.chain(s + 2)
         g.landed(s, 2)
-        scan(s, 2, own)
+        step(s, 2)
         g.cross(s + 1)
         g.landed(s, 4)
         g.landed(s, 3)
-        scan(s, 3, own)
-        for h in range(heads):
-            weigh(s, h, own)
-            if h == heads // 2:
-                g.diagonal(s + 1)
-
-    scan(0, 0, True)
+        step(s, 3)
+        g.diagonal(s + 1)
+
+    step(0, 0)
     g.chain(1)
     g.cross(0)
     g.diagonal(0)
-    one_round(0, True)
-
-    @pl.loop(1, z + 1)
-    def _(s):
-        one_round(s, False)
+    one_round(0)
+    for s in range(1, planes):
+        pl.when(s <= z)(functools.partial(one_round, s))
+    for s in range(planes):
+
+        @pl.when(s == z)
+        def _():
+            for h in range(heads):
+                weigh(s, h)
 
     for h in range(heads):
         inverse = 1.0 / acc[h, :, HD:]
@@ -277,7 +294,7 @@
     out_copy = pltpu.make_async_copy(o_ref, rows_hbm, store.at[0])
     out_copy.start()
     across = jnp.transpose(comb[...])
-    held_rows = mx_ref
+    held_rows = mx_ref.at[0]
     for half in range(tok // HD):
         held_rows[0, half * HD : (half + 1) * HD, :] = across[:, half * HD : (half + 1) * HD]
     line = lax.broadcasted_iota(jnp.int32, (16, tok), 0)
@@ -354,9 +371,9 @@
             pltpu.VMEM(queries.shape, jnp.bfloat16),
             pltpu.VMEM((ctx, cores, 2, width, HD), jnp.bfloat16),
             pltpu.VMEM((heads, tok, 2 * HD), jnp.bfloat16),
-            pltpu.VMEM((heads, tok, PLANE * tok), jnp.float32),
+            pltpu.VMEM((2, heads, tok, PLANE * tok), jnp.float32),
             pltpu.VMEM((planes, heads, tok, PLANE * tok), jnp.bfloat16),
-            pltpu.VMEM((heads, tok, HD), jnp.float32),
+            pltpu.VMEM((2, heads, tok, HD), jnp.float32),
             pltpu.VMEM((planes, heads, tok, HD), jnp.float32),
             pltpu.VMEM((heads, tok, 2 * HD), jnp.float32),
             pltpu.VMEM(queries.shape, jnp.bfloat16),

time: 42.2 us -> 42 us (level)
  no operation moved by 1% of the time
where the time goes in v1:
time: 42 us; the launch traced here: 41.8 us
  Pallas kernels  39 us (93%)
  local copies, waits for them, and re-layouts  2.19 us (5%)
  between operations  0.65 us (2%)
    pallas_call x1, Pallas kernels, body(): pl.pallas_call(functools.partial(kernel, planes, cores), out_shape=(jax.S...  39 us
    unnamed x4, local copies, waits for them, and re-layouts  2.19 us

profile of v1, /device:TPU:0, one launch (start us, length us, event | category | flops | bytes accessed | tf_op | source)
XLA Modules:
  0.0 41.8 jit_solution(16770066828833658433)
XLA Ops:
  0.6 39.0 %attend.1 = (bf16[256,512]{1,0:T(8,128)(2,1)}, f32[1,128]{1,0:T(1,128)}) custom-call(s32[4]{0:T(128)} %docs_ref.1, bf16[256,512]{1,0:T(8,128)(2,1)} %q_hbm.1, bf16[256,128]{1,0:T(8,128)(2,1)} %k_hbm.1, bf16[256,128]{1,0:T(8,128)(2,1)} %v_hbm.1), custom_call_target="tpu_custom_call" | custom-call | tf_op jit(solution)/shard_map/attend/pallas_call | solution.py:362
  39.6 0.0 copy-start
  39.6 1.7 %copy.8 = bf16[256,512]{1,0:T(8,128)(2,1)} copy(bf16[256,512]{1,0:T(8,128)(2,1)} %get-tuple-element.8) | data formatting | bytes 524288
  41.3 0.0 copy-done
  41.3 0.5 %copy.9 = f32[128]{0:T(128)} copy(f32[128]{0:T(128)S(1)} %bitcast.1) | data formatting | bytes 1024
Async XLA Ops:
  39.6 1.7 %copy-start = (f32[1,128]{1,0:T(1,128)S(1)}, f32[1,128]{1,0:T(1,128)}, u32[]{:S(2)}) copy-start(f32[1,128]{1,0:T(1,128)} %get-tuple-element.5) | copy-start | bytes 1540

commit v2 on v1

--- a/solution.py
+++ b/solution.py
@@ -257,10 +257,10 @@
             step(s, 0)
         g.landed(s, 1)
         step(s, 1)
-        g.chain(s + 2)
+        g.chain(s + 3)
         g.landed(s, 2)
         step(s, 2)
-        g.cross(s + 1)
+        g.cross(s + 2)
         g.landed(s, 4)
         g.landed(s, 3)
         step(s, 3)
@@ -269,6 +269,8 @@
     step(0, 0)
     g.chain(1)
     g.cross(0)
+    g.chain(2)
+    g.cross(1)
     g.diagonal(0)
     one_round(0)
     for s in range(1, planes):

time: 42 us -> 38.7 us (0.921)
  Pallas kernels: 39 us -> 35.7 us
    pallas_call x1, Pallas kernels: 39 us -> 35.7 us  [body(): pl.pallas_call(functools.partial(kernel, planes, cores), out_shape=(jax.S...]
where the time goes in v2:
time: 38.7 us; the launch traced here: 38.5 us
  Pallas kernels  35.7 us (92%)
  local copies, waits for them, and re-layouts  2.19 us (6%)
  between operations  0.65 us (2%)
    pallas_call x1, Pallas kernels, body(): pl.pallas_call(functools.partial(kernel, planes, cores), out_shape=(jax.S...  35.7 us
    unnamed x4, local copies, waits for them, and re-layouts  2.19 us

profile of v2, /device:TPU:0, one launch (start us, length us, event | category | flops | bytes accessed | tf_op | source)
XLA Modules:
  0.0 38.5 jit_solution(15837561848423291319)
XLA Ops:
  0.6 35.7 %attend.1 = (bf16[256,512]{1,0:T(8,128)(2,1)}, f32[1,128]{1,0:T(1,128)}) custom-call(s32[4]{0:T(128)} %docs_ref.1, bf16[256,512]{1,0:T(8,128)(2,1)} %q_hbm.1, bf16[256,128]{1,0:T(8,128)(2,1)} %k_hbm.1, bf16[256,128]{1,0:T(8,128)(2,1)} %v_hbm.1), custom_call_target="tpu_custom_call" | custom-call | tf_op jit(solution)/shard_map/attend/pallas_call | solution.py:364
  36.3 0.0 copy-start
  36.4 1.7 %copy.8 = bf16[256,512]{1,0:T(8,128)(2,1)} copy(bf16[256,512]{1,0:T(8,128)(2,1)} %get-tuple-element.8) | data formatting | bytes 524288
  38.0 0.0 copy-done
  38.0 0.5 %copy.9 = f32[128]{0:T(128)} copy(f32[128]{0:T(128)S(1)} %bitcast.1) | data formatting | bytes 1024
Async XLA Ops:
  36.3 1.7 %copy-start = (f32[1,128]{1,0:T(1,128)S(1)}, f32[1,128]{1,0:T(1,128)}, u32[]{:S(2)}) copy-start(f32[1,128]{1,0:T(1,128)} %get-tuple-element.5) | copy-start | bytes 1540
